TPU v7x, 128 devices: a whole 4x4x4 slice. The times are simulated.
128 devices in a mesh: dp: 4 (over y), tensor: 32 (over x, z, core).
Axes of the slice: x: 4, y: 4, z: 4, core: 2. Of those that a mesh axis runs over, the one named last changes fastest.
Arguments:
- hidden_input: bfloat16 [4096, 29568], P('dp', 'tensor'), may hold values from -6 to 6
- output_gradient: bfloat16 [4096, 8192], P('dp', 'tensor'), may hold values from -6 to 6
- frozen_weight: bfloat16 [29568, 8192], P('tensor'), may hold values from -0.03125 to 0.03125
- adapter_down: float32 [29568, 128], P('tensor'), may hold values from -0.773465 to 0.773465, as said below
- adapter_up: float32 [128, 8192], P(None, 'tensor'), may hold values from -1.4694563 to 1.4694563, as said below
Outputs:
- input_grad: bfloat16 [4096, 29568], P('dp', 'tensor')
- step_down: float32 [29568, 128], P('tensor')
- step_up: float32 [128, 8192], P(None, 'tensor')
Inputs may be any that keep to these rules, and one draw needn't show every extreme that they name: `adapter_down`: a trained adapter factor. `adapter_up`: a trained adapter factor.
All inputs are finite; a program needn't handle non-finite values.
Results may differ from a plain program's by a relative error of at most 0.0064.
Values may be sent and summed in bfloat16 or wider, within the bound.
A program may use at most 128 MiB of HBM per device.

v0:
```python
import jax
import jax.numpy as jnp
from jax import lax
from jax.sharding import PartitionSpec as P

SCALE = 2.0
RATE = 0.01
DAMPING = 0.01


def contract(left, right, dims_left, dims_right):
    return lax.dot_general(
        left, right, (((dims_left,), (dims_right,)), ((), ())), preferred_element_type=jnp.float32
    )


def precondition(chol_up, chol_down, grad_down, grad_up):
    step_down = RATE * jax.scipy.linalg.cho_solve((chol_up, True), grad_down.T).T
    step_up = RATE * jax.scipy.linalg.cho_solve((chol_down, True), grad_up)
    return (step_down, step_up)


def per_device(hidden_input, output_gradient, frozen_weight, adapter_down, adapter_up):
    down_factor_half = adapter_down.astype(jnp.bfloat16)
    up_factor_half = adapter_up.astype(jnp.bfloat16)
    adapter_rank = adapter_down.shape[1]
    input_partial = jnp.dot(hidden_input, down_factor_half, preferred_element_type=jnp.float32)
    down_gram_piece = jnp.dot(adapter_down.T, adapter_down, precision=lax.Precision.HIGHEST)
    cotangent_partial = contract(output_gradient, up_factor_half, 1, 1)
    up_gram_piece = jnp.dot(adapter_up, adapter_up.T, precision=lax.Precision.HIGHEST)
    rank_input, rank_cotangent, down_gram_matrix, up_gram_matrix = lax.psum(
        (input_partial, cotangent_partial, down_gram_piece, up_gram_piece), "tensor"
    )
    base_term = contract(
        lax.all_gather(output_gradient, "tensor", axis=1, tiled=True), frozen_weight, 1, 1
    )
    input16 = rank_input.astype(jnp.bfloat16)
    cotangent16 = rank_cotangent.astype(jnp.bfloat16)
    input_grad = (base_term + SCALE * contract(cotangent16, down_factor_half, 1, 1)).astype(
        jnp.bfloat16
    )
    grad_down_partial = SCALE * contract(hidden_input, cotangent16, 0, 0)
    grad_up_partial = SCALE * contract(input16, output_gradient, 0, 0)
    identity = jnp.eye(adapter_rank, dtype=jnp.float32)
    chol_up = jnp.linalg.cholesky(up_gram_matrix + DAMPING * identity)
    chol_down = jnp.linalg.cholesky(down_gram_matrix + DAMPING * identity)
    grad_down, grad_up = lax.psum((grad_down_partial, grad_up_partial), "dp")
    step_down, step_up = precondition(chol_up, chol_down, grad_down, grad_up)
    return (input_grad, step_down, step_up)


def solution(mesh):
    in_specs = (
        P("dp", "tensor"),
        P("dp", "tensor"),
        P("tensor", None),
        P("tensor", None),
        P(None, "tensor"),
    )
    out_specs = (P("dp", "tensor"), P("tensor", None), P(None, "tensor"))
    return jax.shard_map(
        per_device, mesh=mesh, in_specs=in_specs, out_specs=out_specs, check_vma=False
    )
```

profile of v0, /device:TPU:1, one launch (start us, length us, event | category | flops | bytes accessed | tf_op | source)
XLA Modules:
  0.0 317.4 jit_solution(7972166169410403826)
XLA Ops:
  7.2 2.0 fusion.20
  9.3 2.8 fusion.21
  12.2 2.6 fusion.5
  15.1 136.7 %all-reduce.10 = (bf16[1024,128]{1,0:T(8,128)(2,1)}, bf16[1024,128]{1,0:T(8,128)(2,1)}) all-reduce(f32[1024,128]{1,0:T(8,128)S(1)} %fusion.18, f32[1024,128]{1,0:T(8,128)} %fusion.5), channel_id=1, replica_groups=mesh['dp'=4,'tensor'=32] {'tensor'}, use_global_device_ids=true, to_apply=%region_0.0 | all-reduce | flops 262144 | bytes 1572864 | tf_op jit(solution)/shard_map/psum | solution.py:31
  151.8 2.6 fusion
  154.3 1.9 convolution_multiply_fusion.2
  157.0 2.5 fusion.3
  159.5 0.9 select_add_fusion
  160.4 0.9 fusion.13
  161.4 11.7 %cholesky.55 = f32[128,128]{1,0:T(8,128)S(1)} custom-call(f32[128,128]{1,0:T(8,128)S(1)} %copy.11), custom_call_target="Cholesky" | custom-call | tf_op jit(solution)/shard_map/jit(cholesky)/cholesky | solution.py:46
  173.2 0.6 compare_reduce_fusion
  173.8 0.7 fusion.9
  174.5 9.8 %custom-call.17 = f32[1,128,128]{1,2,0:T(8,128)S(1)} custom-call(f32[1,128,128]{2,1,0:T(8,128)S(1)} %fusion.9), custom_call_target="InvertDiagBlocksLowerTriangular" | custom-call | tf_op jit(solution)/shard_map/jit(_cho_solve)/triangular_solve | solution.py:19
  184.4 0.9 fusion.17
  185.3 11.7 %cholesky.44 = f32[128,128]{1,0:T(8,128)S(1)} custom-call(f32[128,128]{1,0:T(8,128)S(1)} %copy.9), custom_call_target="Cholesky" | custom-call | tf_op jit(solution)/shard_map/jit(cholesky)/cholesky | solution.py:45
  197.1 0.6 compare_reduce_fusion.1
  197.7 0.7 fusion.8
  198.4 10.0 %custom-call.16 = f32[1,128,128]{1,2,0:T(8,128)S(1)} custom-call(f32[1,128,128]{2,1,0:T(8,128)S(1)} %fusion.8), custom_call_target="InvertDiagBlocksLowerTriangular" | custom-call | tf_op jit(solution)/shard_map/jit(_cho_solve)/triangular_solve | solution.py:18
  208.4 1.2 fusion.11
  209.6 0.9 convolution_multiply_fusion.3
  210.6 1.7 fusion.15
  212.2 1.7 convolution_multiply_fusion.1
  214.0 72.6 %all-gather.2.cloned.1.call-done = bf16[1024,8192]{1,0:T(8,128)(2,1)} async-done(((bf16[1024,256]{1,0:T(8,128)(2,1)}), bf16[1024,8192]{1,0:T(8,128)(2,1)}) %all-gather.2.cloned.1.call-update) | async-done | bytes 16777232 | tf_op jit(solution)/shard_map/all_gather | solution.py:35
  286.6 24.2 %add_convert_fusion = bf16[1024,924]{0,1:T(8,128)(2,1)} fusion(f32[1024,924]{0,1:T(8,128)} %fusion.3, bf16[1024,8192]{1,0:T(8,128)(2,1)} %all-gather.2.cloned.1.call-done, bf16[924,8192]{1,0:T(8,128)(2,1)} %param.8), kind=kOutput, calls=%fused_computation | convolution fusion | flops 15504986112 | bytes 37593088 | tf_op jit(solution)/shard_map/dot_general | solution.py:12
  (25 shorter events, 1.6 us)
Async XLA Ops:
  7.2 5.0 %copy-start = (bf16[1024,924]{0,1:T(8,128)(2,1)S(1)}, bf16[1024,924]{0,1:T(8,128)(2,1)}, u32[]{:S(2)}) copy-start(bf16[1024,924]{0,1:T(8,128)(2,1)} %param.6) | copy-start | bytes 5677060
  7.2 7.6 %copy-start.3 = (f32[128,256]{1,0:T(8,128)S(1)}, f32[128,256]{1,0:T(8,128)}, u32[]{:S(2)}) copy-start(f32[128,256]{1,0:T(8,128)} %param.10) | copy-start | bytes 393220
  7.2 7.6 %copy-start.2 = (bf16[1024,256]{1,0:T(8,128)(2,1)S(1)}, bf16[1024,256]{1,0:T(8,128)(2,1)}, u32[]{:S(2)}) copy-start(bf16[1024,256]{1,0:T(8,128)(2,1)} %param.7) | copy-start | bytes 1572868
  7.2 152.3 %all-reduce.7.cloned.1.call-start = ((), (), s32[]{:S(2)}) async-start(), calls=%async_computation.1 | async-start | bytes 262144 | tf_op jit(solution)/shard_map/psum | solution.py:31
  12.1 196.3 %all-reduce.9.cloned.1.call-start = ((), (), s32[]{:S(2)}) async-start(), calls=%async_computation.2 | async-start | bytes 1310720 | tf_op jit(solution)/shard_map/psum | solution.py:47
  14.8 142.2 %copy-start.1 = (f32[924,128]{1,0:T(8,128)S(1)}, f32[924,128]{1,0:T(8,128)}, u32[]{:S(2)}) copy-start(f32[924,128]{1,0:T(8,128)} %param.9) | copy-start | bytes 1419268
  151.7 5.2 %copy-start.4 = (bf16[1024,128]{1,0:T(8,128)(2,1)S(1)}, bf16[1024,128]{1,0:T(8,128)(2,1)}, u32[]{:S(2)}) copy-start(bf16[1024,128]{1,0:T(8,128)(2,1)} %get-tuple-element.4) | copy-start | bytes 786436
  156.2 130.4 %all-gather.2.cloned.1.call-start = ((), (), s32[]{:S(2)}) async-start(), calls=%async_computation | async-start | bytes 17301504 | tf_op jit(solution)/shard_map/all_gather | solution.py:35
Sparse Core Ops, SparseCore 0:
  12.3 103.2 all-reduce.6
  156.3 43.9 all-reduce.8
  202.8 83.8 all-gather.1
where the time goes:
time: 318 us; the launch traced here: 317 us
  blocking collectives  137 us (43%)
  waiting for transfers between devices  73.2 us (23%)
  other arithmetic  48.5 us (15%)
  matrix products  44.4 us (14%)
  between operations  13.9 us (4%)
    psum x1, blocking collectives, per_device(): lax.psum((input_partial, cotangent_partial, down_gram_piece, up_gram_piec...  137 us
    all_gather x1, waiting for transfers between devices, per_device(): lax.all_gather(output_gradient, 'tensor', axis=1, tiled=True)  72.6 us
    dot_general x5, matrix products, contract(): lax.dot_general(left, right, (((dims_left,), (dims_right,)), ((), ())), p...  31.4 us
    another operation x3, other arithmetic, per_device(): chol_up = jnp.linalg.cholesky(up_gram_matrix + DAMPING * identity)  12.4 us
    another operation x3, other arithmetic, per_device(): chol_down = jnp.linalg.cholesky(down_gram_matrix + DAMPING * identity)  12.4 us
    another operation x2, other arithmetic, precondition(): jax.scipy.linalg.cho_solve((chol_up, True), grad_down.T)  10.6 us
    another operation x2, other arithmetic, precondition(): step_up = RATE * jax.scipy.linalg.cho_solve((chol_down, True), grad_up)  10.5 us
  transfers between devices with their start and end apart: 3, of which 1 were waited for; matrix products, arithmetic and copies ran while one was open for 20% of the time, Pallas kernels for 0%

commit v1 on v0

v1 whole, which is shorter than its diff:
```python
import jax
import jax.numpy as jnp
from jax import lax
from jax.experimental import pallas as pl
from jax.experimental.pallas import tpu as pltpu
from jax.sharding import PartitionSpec as P

SCALE = 2.0
RATE = 0.01
DAMPING = 0.01
RANK = 128
TOKENS = 1024
COLS = 256
HIDDEN = 924
SLOTS = 32
CHUNKS = 2
CHUNK = TOKENS // CHUNKS
DOWN_ROWS, UP_ROWS = 232, 64
STEP_ROWS = DOWN_ROWS + UP_ROWS
BLOCK = 72
MESH = pl.DeviceIdType.MESH
HIGHEST = lax.Precision.HIGHEST

ORDER = (
    (0, 0), (-1, 0), (1, 0), (0, -1), (0, 1), (2, 0), (0, 2), (-1, -1), (-1, 1),
    (-1, 2), (1, -1), (1, 1), (1, 2), (2, -1), (2, 1), (2, 2),
)
OWN_AT = {1: 0, 2: 0, 3: 2, 4: 2, 5: 3, 6: 4, 7: 5, 8: 6, 9: 7, 10: 8, 11: 9, 12: 10, 13: 12, 14: 13, 15: 14}
INVERT_FROM, INVERT_PER = 5, 2
STEPS = 16


def dot(left, right, dims_left, dims_right, precision=None):
    return lax.dot_general(
        left,
        right,
        (((dims_left,), (dims_right,)), ((), ())),
        precision=precision,
        preferred_element_type=jnp.float32,
    )


def eliminate(mat, count):
    lane = lax.broadcasted_iota(jnp.int32, (RANK, RANK), 1)
    row_of = lax.broadcasted_iota(jnp.int32, (RANK, RANK), 0)
    lane_row = lax.broadcasted_iota(jnp.int32, (1, RANK), 1)
    for j in range(count):
        column = jnp.broadcast_to(mat[:, j : j + 1], (RANK, RANK))
        inverse = 1.0 / column[j : j + 1, :]
        row = jnp.where(lane_row == j, inverse, mat[j : j + 1, :] * inverse)
        base = jnp.where((lane == j) | (row_of == j), 0.0, mat)
        mat = base - jnp.where(row_of == j, -1.0, column) * row
    mat = jnp.concatenate([mat[count:], mat[:count]], axis=0)
    return pltpu.roll(mat, RANK - count, axis=1)


def kernel(
    hidden_hbm, grad_hbm, weight_hbm, down_hbm, up_hbm,
    out_hbm, step_down_hbm, step_up_hbm,
    buf, weight, hidden, down, up, down16, acc, out16,
    part, from_sib, chip_sum, ring1, quarter, ring2, half16, gram,
    inverse, grads, grads_in, steps, step_up,
    local_sem, send_sem, slot_sem, misc_sem,
):
    dp = lax.axis_index("dp")
    me = lax.axis_index("tensor")
    core = lax.rem(me, 2)
    z = lax.rem(me // 2, 4)
    x = me // 8
    other = 1 - core
    a = x + core * (z - x)
    b = z + core * (x - z)

    def mod4(v):
        return lax.rem(v + 8, 4)

    def place(core_, a_, b_):
        return mod4(a_) * (8 - 6 * core_) + mod4(b_) * (2 + 6 * core_) + core_

    sib = me + 1 - 2 * core
    own = [place(core, a + da, b + db) for da, db in ORDER]
    theirs = [place(other, b + da, a + db) for da, db in ORDER]
    along_a = [(dp, place(core, a + d, b)) for d in (1, -1, 2)]
    along_b = [(dp, place(core, a, b + d)) for d in (1, -1, 2)]
    along_y = [(mod4(dp + d), me) for d in (1, -1, 2)]
    sibling = (dp, sib)
    a_plus, a_minus = along_a[0], along_a[1]
    b_plus, b_minus = along_b[0], along_b[1]

    def local(src, dst, sem):
        return pltpu.make_async_copy(src, dst, local_sem.at[sem])

    loads = [
        local(grad_hbm, buf.at[me], 0),
        local(up_hbm, up, 1),
        local(hidden_hbm, hidden, 2),
        local(down_hbm, down, 3),
        local(weight_hbm, weight, 4),
    ]
    for load in loads:
        load.start()

    barrier = pltpu.get_barrier_semaphore()
    partners = along_a + along_b + along_y + [sibling]
    for partner in partners:
        pl.semaphore_signal(barrier, inc=1, device_id=partner, device_id_type=MESH)
    pl.semaphore_wait(barrier, len(partners))

    pending = []

    def remote(refs, device):
        index = len(pending)

        def make(device):
            src, dst, recv_sem = refs()
            return pltpu.make_async_remote_copy(
                src_ref=src,
                dst_ref=dst,
                send_sem=send_sem.at[index],
                recv_sem=recv_sem,
                device_id=device,
                device_id_type=MESH,
            )

        pending.append(make)
        make(device).start()

    def landed(dst, recv_sem):
        pltpu.make_async_remote_copy(
            src_ref=dst,
            dst_ref=dst,
            send_sem=send_sem.at[0],
            recv_sem=recv_sem,
            device_id=sibling,
            device_id_type=MESH,
        ).wait_recv()

    def piece(slot, c):
        return buf.at[slot, pl.ds(c * CHUNK, CHUNK)]

    def pass_on(slot, c, device):
        remote(lambda: (piece(slot, c), piece(slot, c), slot_sem.at[slot, c]), device)

    def arrived(slot, c):
        landed(piece(slot, c), slot_sem.at[slot, c])

    SIB_PART, RING1, RING2, AG1_HALF, AG1_GRAM, AG2_HALF, AG2_GRAM = 0, 1, 4, 7, 10, 13, 16
    SIB_HALF, SIB_INV, Y_GRAD, Y_STEP = 19, 20, 21, 24

    loads[0].wait()
    for c in range(CHUNKS):
        pass_on(me, c, a_plus)
        pass_on(me, c, a_minus)

    loads[1].wait()
    up_f32 = up[...]
    part[0, :, 0:64, :] = dot(buf[me], up_f32.astype(jnp.bfloat16), 1, 1).reshape(16, 64, RANK)
    part[0, :, 64:BLOCK, :] = dot(up_f32, up_f32, 1, 1, HIGHEST).reshape(16, 8, RANK)
    loads[2].wait()
    loads[3].wait()
    down_f32 = down[...]
    down16[...] = down_f32.astype(jnp.bfloat16)
    part[1, :, 0:64, :] = dot(hidden[...], down16[...], 1, 0).reshape(16, 64, RANK)
    part[1, :, 64:BLOCK, :] = dot(down_f32, down_f32, 0, 0, HIGHEST).reshape(16, 8, RANK)
    remote(lambda: (part.at[other], from_sib, misc_sem.at[SIB_PART]), sibling)
    for c in range(CHUNKS):
        pass_on(me, c, sibling)
    acc[...] = jnp.zeros_like(acc)
    landed(from_sib, misc_sem.at[SIB_PART])
    for j, (d, device) in enumerate(zip((1, -1, 2, 0), along_a + [None])):
        rows = pl.ds(mod4(a + d) * 4, 4)
        chip_sum[rows] = part[core, rows] + from_sib[rows]
        if device is not None:
            remote(lambda j=j, rows=rows: (chip_sum.at[rows], ring1.at[j], misc_sem.at[RING1 + j]), device)
    pass_on(me, 0, b_plus)
    pass_on(me, 0, b_minus)
    loads[4].wait()

    def reduce_a():
        for j in range(3):
            landed(ring1.at[j], misc_sem.at[RING1 + j])
        quarter[...] = (chip_sum[pl.ds(a * 4, 4)] + ring1[0]) + (ring1[1] + ring1[2])
        for j, (d, device) in enumerate(zip((1, -1, 2), along_b)):
            remote(lambda j=j, d=d: (quarter.at[mod4(b + d)], ring2.at[j], misc_sem.at[RING2 + j]), device)
        pass_on(me, 1, b_plus)
        pass_on(me, 1, b_minus)

    mine = a * 4 + b

    def own_rows():
        return pl.ds(a * 4, 4)

    def reduce_b():
        for j in range(3):
            landed(ring2.at[j], misc_sem.at[RING2 + j])
        total = (quarter[b] + ring2[0]) + (ring2[1] + ring2[2])
        half16[core, mine] = total[0:64].astype(jnp.bfloat16)
        gram[mine] = total[64:BLOCK]
        for j, device in enumerate(along_b):
            remote(lambda j=j: (half16.at[core, mine], half16.at[core, mine], misc_sem.at[AG1_HALF + j]), device)
            remote(lambda j=j: (gram.at[mine], gram.at[mine], misc_sem.at[AG1_GRAM + j]), device)

    def gather_a():
        for j, d in enumerate((1, -1, 2)):
            block = a * 4 + mod4(b - d)
            landed(half16.at[core, block], misc_sem.at[AG1_HALF + j])
            landed(gram.at[block], misc_sem.at[AG1_GRAM + j])
        for j, device in enumerate(along_a):
            remote(lambda j=j: (half16.at[core, own_rows()], half16.at[core, own_rows()], misc_sem.at[AG2_HALF + j]), device)
            remote(lambda j=j: (gram.at[own_rows()], gram.at[own_rows()], misc_sem.at[AG2_GRAM + j]), device)

    def share_sib():
        for j, d in enumerate((1, -1, 2)):
            rows = pl.ds(mod4(a - d) * 4, 4)
            landed(half16.at[core, rows], misc_sem.at[AG2_HALF + j])
            landed(gram.at[rows], misc_sem.at[AG2_GRAM + j])
        remote(lambda: (half16.at[core], half16.at[core], misc_sem.at[SIB_HALF]), sibling)
        eye = lax.broadcasted_iota(jnp.int32, (RANK, RANK), 0) == lax.broadcasted_iota(
            jnp.int32, (RANK, RANK), 1
        )
        inverse[core] = gram[...].reshape(RANK, RANK) + jnp.where(eye, DAMPING, 0.0)

    def form_grads():
        landed(half16.at[other], misc_sem.at[SIB_HALF])
        cotangent16 = half16[0].reshape(TOKENS, RANK)
        input16 = half16[1].reshape(TOKENS, RANK)
        grad_down = SCALE * dot(cotangent16, hidden[...], 0, 0).T
        grad_up = SCALE * dot(input16, buf[me], 0, 0).T
        for q in range(4):
            last = min(DOWN_ROWS, HIDDEN - q * DOWN_ROWS)
            grads[q, 0:last] = grad_down[q * DOWN_ROWS : q * DOWN_ROWS + last]
            if last < DOWN_ROWS:
                grads[q, last:DOWN_ROWS] = jnp.zeros((DOWN_ROWS - last, RANK), jnp.float32)
            grads[q, DOWN_ROWS:STEP_ROWS] = grad_up[q * UP_ROWS : (q + 1) * UP_ROWS]
        for j, (d, device) in enumerate(zip((1, -1, 2), along_y)):
            remote(lambda j=j, d=d: (grads.at[mod4(dp + d)], grads_in.at[j], misc_sem.at[Y_GRAD + j]), device)
        acc[...] += dot(cotangent16 * jnp.bfloat16(SCALE), down16[...], 1, 1)

    def share_inverse():
        remote(lambda: (inverse.at[core], inverse.at[core], misc_sem.at[SIB_INV]), sibling)

    def solve():
        for j in range(3):
            landed(grads_in.at[j], misc_sem.at[Y_GRAD + j])
        total = RATE * ((grads[dp] + grads_in[0]) + (grads_in[1] + grads_in[2]))
        landed(inverse.at[other], misc_sem.at[SIB_INV])
        steps[dp, 0:DOWN_ROWS] = dot(total[0:DOWN_ROWS], inverse[0], 1, 0, HIGHEST)
        steps[dp, DOWN_ROWS:STEP_ROWS] = dot(total[DOWN_ROWS:STEP_ROWS], inverse[1], 1, 0, HIGHEST)
        for j, device in enumerate(along_y):
            remote(lambda j=j: (steps.at[dp], steps.at[dp], misc_sem.at[Y_STEP + j]), device)

    def spread(k):
        for c in range(CHUNKS):
            pass_on(own[k], c, b_plus)
            pass_on(own[k], c, b_minus)

    def receive(k):
        da, db = ORDER[k]
        for c in range(CHUNKS):
            arrived(own[k], c)
            if db == 0 and da == -1 and c == 0:
                pass_on(own[k], c, a_plus)
            if db == 0 and da == 1 and c == 1:
                pass_on(own[k], c, a_minus)
            if db == -1 and c == 0:
                pass_on(own[k], c, b_plus)
            if db == 1 and c == 1:
                pass_on(own[k], c, b_minus)
        if ORDER[k] == (2, 0):
            spread(k)
        for c in range(CHUNKS):
            pass_on(own[k], c, sibling)

    events = {i: [] for i in range(STEPS)}
    events[1].append(reduce_a)
    events[2].append(reduce_b)
    events[2].append(lambda: (spread(1), spread(2)))
    events[3].append(gather_a)
    for k in range(1, 16):
        events[OWN_AT[k]].append(lambda k=k: receive(k))
    events[4].append(share_sib)
    events[5].append(form_grads)
    events[13].append(share_inverse)
    events[14].append(solve)

    def pick(values, i):
        index = values[0]
        for k in range(1, len(values)):
            index = jnp.where(i == k, values[k], index)
        return index

    def step(i, carry):
        for k in range(STEPS):
            if events[k]:

                @pl.when(i == k)
                def _(k=k):
                    for event in events[k]:
                        event()

        slot_own, slot_sib = pick(own, i), pick(theirs, i)
        for c in range(CHUNKS):
            arrived(slot_sib, c)
        cols_own = pl.ds(pl.multiple_of(slot_own * COLS, COLS), COLS)
        cols_sib = pl.ds(pl.multiple_of(slot_sib * COLS, COLS), COLS)
        acc[...] += dot(buf[slot_own], weight[:, cols_own], 1, 1) + dot(
            buf[slot_sib], weight[:, cols_sib], 1, 1
        )

        @pl.when((i >= INVERT_FROM) & (i < INVERT_FROM + 16 // INVERT_PER))
        def _():
            mat = inverse[core]
            for _ in range(INVERT_PER):
                mat = eliminate(mat, 8)
            inverse[core] = mat

        return carry

    lax.fori_loop(0, STEPS, step, 0)

    out16[...] = acc[...].astype(jnp.bfloat16)
    stores = [local(out16, out_hbm, 0)]
    stores[0].start()
    for j, d in enumerate((1, -1, 2)):
        landed(steps.at[mod4(dp - d)], misc_sem.at[Y_STEP + j])
    for q in range(4):
        last = min(DOWN_ROWS, HIDDEN - q * DOWN_ROWS)
        store = local(
            steps.at[q, pl.ds(0, last)], step_down_hbm.at[pl.ds(q * DOWN_ROWS, last)], 1 + q
        )
        store.start()
        stores.append(store)
    step_up[...] = steps[:, DOWN_ROWS:STEP_ROWS, :].reshape(COLS, RANK).T
    stores.append(local(step_up, step_up_hbm, 5))
    stores[-1].start()
    for make in pending:
        make(sibling).wait_send()
    for store in stores:
        store.wait()


def per_device(hidden_input, output_gradient, frozen_weight, adapter_down, adapter_up):
    f32, bf16 = jnp.float32, jnp.bfloat16
    any_space = pl.BlockSpec(memory_space=pl.ANY)
    return pl.pallas_call(
        kernel,
        out_shape=(
            jax.ShapeDtypeStruct((TOKENS, HIDDEN), bf16),
            jax.ShapeDtypeStruct((HIDDEN, RANK), f32),
            jax.ShapeDtypeStruct((RANK, COLS), f32),
        ),
        in_specs=[any_space] * 5,
        out_specs=(any_space,) * 3,
        scratch_shapes=[
            pltpu.VMEM((SLOTS, TOKENS, COLS), bf16),
            pltpu.VMEM((HIDDEN, SLOTS * COLS), bf16),
            pltpu.VMEM((TOKENS, HIDDEN), bf16),
            pltpu.VMEM((HIDDEN, RANK), f32),
            pltpu.VMEM((RANK, COLS), f32),
            pltpu.VMEM((HIDDEN, RANK), bf16),
            pltpu.VMEM((TOKENS, HIDDEN), f32),
            pltpu.VMEM((TOKENS, HIDDEN), bf16),
            pltpu.VMEM((2, 16, BLOCK, RANK), f32),
            pltpu.VMEM((16, BLOCK, RANK), f32),
            pltpu.VMEM((16, BLOCK, RANK), f32),
            pltpu.VMEM((3, 4, BLOCK, RANK), f32),
            pltpu.VMEM((4, BLOCK, RANK), f32),
            pltpu.VMEM((3, BLOCK, RANK), f32),
            pltpu.VMEM((2, 16, 64, RANK), bf16),
            pltpu.VMEM((16, 8, RANK), f32),
            pltpu.VMEM((2, RANK, RANK), f32),
            pltpu.VMEM((4, STEP_ROWS, RANK), f32),
            pltpu.VMEM((3, STEP_ROWS, RANK), f32),
            pltpu.VMEM((4, STEP_ROWS, RANK), f32),
            pltpu.VMEM((RANK, COLS), f32),
            pltpu.SemaphoreType.DMA((6,)),
            pltpu.SemaphoreType.DMA((128,)),
            pltpu.SemaphoreType.DMA((SLOTS, CHUNKS)),
            pltpu.SemaphoreType.DMA((27,)),
        ],
        compiler_params=pltpu.CompilerParams(
            collective_id=0, has_side_effects=True, vmem_limit_bytes=60 * 2**20
        ),
    )(hidden_input, output_gradient, frozen_weight, adapter_down, adapter_up)


def solution(mesh):
    in_specs = (
        P("dp", "tensor"),
        P("dp", "tensor"),
        P("tensor", None),
        P("tensor", None),
        P(None, "tensor"),
    )
    out_specs = (P("dp", "tensor"), P("tensor", None), P(None, "tensor"))
    return jax.shard_map(
        per_device, mesh=mesh, in_specs=in_specs, out_specs=out_specs, check_vma=False
    )
```

time: 318 us -> 104 us (0.33)
  blocking collectives: 137 us -> 0 us
  Pallas kernels: 0 us -> 91.7 us
  waiting for transfers between devices: 73.2 us -> 0 us
  other arithmetic: 48.5 us -> 0 us
  matrix products: 44.4 us -> 0 us
  between operations: 13.9 us -> 0.66 us
  local copies, waits for them, and re-layouts: 0.38 us -> 9.26 us
    psum x1 -> x0, blocking collectives: 137 us -> none  [per_device(): lax.psum((input_partial, cotangent_partial, down_gram_piece, up_gram_piec...]
    pallas_call x0 -> x1, Pallas kernels: none -> 91.7 us  [per_device(): pl.pallas_call(kernel, out_shape=(jax.ShapeDtypeStruct((TOKENS, HIDDEN),...]
    all_gather x1 -> x0, waiting for transfers between devices: 72.6 us -> none  [per_device(): lax.all_gather(output_gradient, 'tensor', axis=1, tiled=True)]
    another operation x10 -> x0, other arithmetic: 45.9 us -> none  [the longest x3 12.4 us: per_device(): chol_up = jnp.linalg.cholesky(up_gram_matrix + DAMPING * identity)]
    dot_general x8 -> x0, matrix products: 38.9 us -> none  [the longest x5 31.4 us: contract(): lax.dot_general(left, right, (((dims_left,), (dims_right,)), ((), ())), p...]
    another operation x4 -> x0, matrix products: 5.54 us -> none  [the longest x2 3.41 us: precondition(): jax.scipy.linalg.cho_solve((chol_up, True), grad_down.T)]
    unnamed x10 -> x7, local copies, waits for them, and re-layouts: 0.03 us -> 5.3 us
    pallas_call x0 -> x1, local copies, waits for them, and re-layouts: none -> 3.97 us  [per_device(): pl.pallas_call(kernel, out_shape=(jax.ShapeDtypeStruct((TOKENS, HIDDEN),...]
  transfers between devices with their start and end apart: 3 -> 0, of which waited for: 1 -> 0; matrix products, arithmetic and copies ran while one was open for 20% -> 0% of each run, Pallas kernels for 0% -> 0%
where the time goes in v1:
time: 104 us; the launch traced here: 102 us
  Pallas kernels  91.7 us (88%)
  local copies, waits for them, and re-layouts  9.26 us (9%)
    pallas_call x1, Pallas kernels, per_device(): pl.pallas_call(kernel, out_shape=(jax.ShapeDtypeStruct((TOKENS, HIDDEN),...  91.7 us
    unnamed x7, local copies, waits for them, and re-layouts  5.3 us
    pallas_call x1, local copies, waits for them, and re-layouts, per_device(): pl.pallas_call(kernel, out_shape=(jax.ShapeDtypeStruct((TOKENS, HIDDEN),...  3.97 us

profile of v1, /device:TPU:1, one launch (start us, length us, event | category | flops | bytes accessed | tf_op | source)
XLA Modules:
  0.0 101.6 jit_solution(14081142450115230245)
XLA Ops:
  0.6 3.9 %copy.8.hidden_hbm = bf16[1024,924]{1,0:T(8,128)(2,1)} copy(bf16[1024,924]{0,1:T(8,128)(2,1)} %param.5) | data formatting | bytes 3784704 | tf_op args[0]
  4.5 91.7 %shard_map.76 = (bf16[1024,924]{1,0:T(8,128)(2,1)}, f32[924,128]{1,0:T(8,128)}, f32[128,256]{1,0:T(8,128)}) custom-call(bf16[1024,924]{1,0:T(8,128)(2,1)} %copy.8.hidden_hbm, bf16[1024,256]{1,0:T(8,128)(2,1)} %grad_hbm.1, bf16[924,8192]{1,0:T(8,128)(2,1)} %weight_hbm.1, f32[924,128]{1,0:T(8,128)} %down_hbm.1, f32[128,256]{1,0:T(8,128)} %up_hbm.1), custom_call_target="tpu_custom_call" | custom-call | tf_op jit(solution)/shard_map/pallas_call | solution.py:345
  96.2 0.0 copy-start
  96.2 0.0 copy-start.1
  96.2 4.0 %copy.9 = bf16[1024,924]{0,1:T(8,128)(2,1)} copy(bf16[1024,924]{1,0:T(8,128)(2,1)} %get-tuple-element.3) | data formatting | bytes 3784704 | tf_op jit(solution)/shard_map/pallas_call | solution.py:345
  100.2 0.0 copy-done
  100.2 0.8 copy.12
  101.0 0.0 copy-done.1
  101.0 0.7 copy.13
Async XLA Ops:
  96.2 4.0 %copy-start = (f32[924,128]{1,0:T(8,128)S(1)}, f32[924,128]{1,0:T(8,128)}, u32[]{:S(2)}) copy-start(f32[924,128]{1,0:T(8,128)} %get-tuple-element.10) | copy-start | bytes 1419268
  96.2 4.8 %copy-start.1 = (f32[128,256]{1,0:T(8,128)S(1)}, f32[128,256]{1,0:T(8,128)}, u32[]{:S(2)}) copy-start(f32[128,256]{1,0:T(8,128)} %get-tuple-element.11) | copy-start | bytes 393220

commit v2 on v1

v2 whole, which is shorter than its diff:
```python
import jax
import jax.numpy as jnp
from jax import lax
from jax.experimental import pallas as pl
from jax.experimental.pallas import tpu as pltpu
from jax.sharding import PartitionSpec as P

SCALE = 2.0
RATE = 0.01
DAMPING = 0.01
RANK = 128
TOKENS = 1024
COLS = 256
HIDDEN = 924
SLOTS = 32
CHUNKS = 2
CHUNK = TOKENS // CHUNKS
DOWN_ROWS, UP_ROWS = 240, 64
STEP_ROWS = DOWN_ROWS + UP_ROWS
BLOCK = 64
GRAM_ROWS = 32
MESH = pl.DeviceIdType.MESH
HIGHEST = lax.Precision.HIGHEST

ORDER = (
    (0, 0), (-1, 0), (1, 0), (2, 0), (0, -1), (0, 1), (-1, -1), (-1, 1), (1, -1), (1, 1),
    (0, 2), (2, -1), (2, 1), (-1, 2), (1, 2), (2, 2),
)
LAST = 15
PRODUCTS = (
    (0, 0), (1, 0), (0, 1), (0, 2), (1, 1), (1, 2), (0, 3), (1, 3), (0, 4), (0, 5), (1, 4), (1, 5),
    (0, 6), (0, 7), (1, 6), (1, 7), (0, 8), (0, 9), (1, 8), (1, 9), (0, 10), (1, 10),
    (0, 11), (0, 12), (1, 11), (1, 12), (0, 13), (1, 13), (0, 14), (1, 14),
)
INVERT_FROM, INVERT_TO = 10, 26


def dot(left, right, dims_left, dims_right, precision=None):
    return lax.dot_general(
        left,
        right,
        (((dims_left,), (dims_right,)), ((), ())),
        precision=precision,
        preferred_element_type=jnp.float32,
    )


def eliminate(mat, count):
    lane = lax.broadcasted_iota(jnp.int32, (RANK, RANK), 1)
    row_of = lax.broadcasted_iota(jnp.int32, (RANK, RANK), 0)
    lane_row = lax.broadcasted_iota(jnp.int32, (1, RANK), 1)
    for j in range(count):
        column = jnp.broadcast_to(mat[:, j : j + 1], (RANK, RANK))
        inverse = 1.0 / column[j : j + 1, :]
        row = jnp.where(lane_row == j, inverse, mat[j : j + 1, :] * inverse)
        base = jnp.where((lane == j) | (row_of == j), 0.0, mat)
        mat = base - jnp.where(row_of == j, -1.0, column) * row
    mat = jnp.concatenate([mat[count:], mat[:count]], axis=0)
    return pltpu.roll(mat, RANK - count, axis=1)


def kernel(
    hidden_hbm, grad_hbm, weight_hbm, down_hbm, up_hbm,
    out_hbm, step_down_hbm, step_up_hbm,
    buf, weight, hidden, down, up, down16, acc, out16,
    part, from_sib, chip_sum, ring1, quarter, ring2, sum16, half16,
    gram_part, gram_sib, gram_sum, gram_in, gram,
    inverse, grads, grads_in, steps, step_down, step_up,
    local_sem, send_sem, slot_sem, misc_sem,
):
    dp = lax.axis_index("dp")
    me = lax.axis_index("tensor")
    core = lax.rem(me, 2)
    z = lax.rem(me // 2, 4)
    x = me // 8
    other = 1 - core
    a = x + core * (z - x)
    b = z + core * (x - z)

    def mod4(v):
        return lax.rem(v + 8, 4)

    def place(core_, a_, b_):
        return mod4(a_) * (8 - 6 * core_) + mod4(b_) * (2 + 6 * core_) + core_

    sib = me + 1 - 2 * core
    own = [place(core, a + da, b + db) for da, db in ORDER]
    theirs = [place(other, b + da, a + db) for da, db in ORDER]
    along_a = [(dp, place(core, a + d, b)) for d in (1, -1, 2)]
    along_b = [(dp, place(core, a, b + d)) for d in (1, -1, 2)]
    along_y = [(mod4(dp + d), me) for d in (1, -1, 2)]
    sibling = (dp, sib)
    a_plus, a_minus = along_a[0], along_a[1]
    b_plus, b_minus = along_b[0], along_b[1]

    def local(src, dst, sem):
        return pltpu.make_async_copy(src, dst, local_sem.at[sem])

    loads = [
        local(grad_hbm, buf.at[me], 0),
        local(up_hbm, up, 1),
        local(hidden_hbm, hidden, 2),
        local(down_hbm, down, 3),
        local(weight_hbm, weight, 4),
    ]
    for load in loads[:4]:
        load.start()

    barrier = pltpu.get_barrier_semaphore()
    cross_a = [(dp, place(other, b, a + d)) for d in (1, -1, 2)]
    cross_b = [(dp, place(other, b + d, a)) for d in (1, -1, 2)]
    partners = along_a + along_b + along_y + [sibling] + cross_a + cross_b
    for partner in partners:
        pl.semaphore_signal(barrier, inc=1, device_id=partner, device_id_type=MESH)

    pending = []

    def remote(refs, device):
        index = len(pending)

        def make(device):
            src, dst, recv_sem = refs()
            return pltpu.make_async_remote_copy(
                src_ref=src,
                dst_ref=dst,
                send_sem=send_sem.at[index],
                recv_sem=recv_sem,
                device_id=device,
                device_id_type=MESH,
            )

        pending.append(make)
        make(device).start()

    def landed(dst, recv_sem):
        pltpu.make_async_remote_copy(
            src_ref=dst,
            dst_ref=dst,
            send_sem=send_sem.at[0],
            recv_sem=recv_sem,
            device_id=sibling,
            device_id_type=MESH,
        ).wait_recv()

    def piece(slot, c):
        return buf.at[slot, pl.ds(c * CHUNK, CHUNK)]

    def pass_on(slot, c, device):
        remote(lambda: (piece(slot, c), piece(slot, c), slot_sem.at[slot, c]), device)

    def arrived(slot, c):
        landed(piece(slot, c), slot_sem.at[slot, c])

    SIB_PART, RING1, RING2, AG1, AG2, SIB_HALF, SIB_INV, Y_GRAD, Y_STEP = 0, 1, 5, 8, 12, 15, 16, 17, 20
    GRAM_SIB, GRAM_1, GRAM_Y = 23, 24, 32

    def own_first(c):
        pass_on(me, c, a_plus)
        pass_on(me, c, a_minus)

    loads[0].wait()
    loads[1].wait()
    up_f32 = up[...]
    part[0] = dot(buf[me], up_f32.astype(jnp.bfloat16), 1, 1).reshape(16, BLOCK, RANK)
    gram_part[0] = dot(up_f32, up_f32, 1, 1, HIGHEST).reshape(4, GRAM_ROWS, RANK)
    loads[2].wait()
    loads[3].wait()
    loads[4].start()
    down_f32 = down[...]
    down16[...] = down_f32.astype(jnp.bfloat16)
    gram_part[1] = dot(down_f32, down_f32, 0, 0, HIGHEST).reshape(4, GRAM_ROWS, RANK)
    part[1] = dot(down16[...], hidden[...], 0, 0).T.reshape(16, BLOCK, RANK)
    pl.semaphore_wait(barrier, len(partners))
    remote(lambda: (gram_part.at[other, dp], gram_sib, misc_sem.at[GRAM_SIB]), sibling)
    remote(lambda: (part.at[other], from_sib, misc_sem.at[SIB_PART]), sibling)
    own_first(0)
    own_first(1)
    for c in range(CHUNKS):
        pass_on(me, c, sibling)
    acc[...] = jnp.zeros_like(acc)

    def gram_stage(n, value):
        gram_sum[n] = value
        for j, device in enumerate(cross_b + [sibling]):
            remote(lambda j=j: (gram_sum.at[n], gram_in.at[n, j], misc_sem.at[GRAM_1 + 4 * n + j]), device)

    def gram_total(n):
        for j in range(4):
            landed(gram_in.at[n, j], misc_sem.at[GRAM_1 + 4 * n + j])
        return (gram_in[n, 0] + gram_in[n, 1]) + (gram_in[n, 2] + gram_in[n, 3])

    landed(gram_sib, misc_sem.at[GRAM_SIB])
    gram_stage(0, gram_part[core, dp] + gram_sib[...])
    landed(from_sib, misc_sem.at[SIB_PART])
    for j, (d, device) in enumerate(zip((1, -1, 2, 0), cross_a + [sibling])):
        rows = pl.ds(mod4(a + d) * 4, 4)
        chip_sum[rows] = part[core, rows] + from_sib[rows]
        remote(lambda j=j, rows=rows: (chip_sum.at[rows], ring1.at[j], misc_sem.at[RING1 + j]), device)

    def gram_first():
        gram_stage(1, gram_total(0))
        for c in range(CHUNKS):
            pass_on(me, c, b_plus)
            pass_on(me, c, b_minus)

    def gram_second():
        gram[dp] = gram_total(1)
        for j, device in enumerate(along_y):
            remote(lambda j=j: (gram.at[dp], gram.at[dp], misc_sem.at[GRAM_Y + j]), device)

    def gram_third():
        for j, d in enumerate((1, -1, 2)):
            landed(gram.at[mod4(dp - d)], misc_sem.at[GRAM_Y + j])
        eye = lax.broadcasted_iota(jnp.int32, (RANK, RANK), 0) == lax.broadcasted_iota(
            jnp.int32, (RANK, RANK), 1
        )
        inverse[core] = gram[...].reshape(RANK, RANK) + jnp.where(eye, DAMPING, 0.0)

    def reduce_first():
        for j in range(4):
            landed(ring1.at[j], misc_sem.at[RING1 + j])
        quarter[...] = (ring1[3] + ring1[0]) + (ring1[1] + ring1[2])
        for j, (d, device) in enumerate(zip((1, -1, 2), along_a)):
            remote(lambda j=j, d=d: (quarter.at[mod4(a + d)], ring2.at[j], misc_sem.at[RING2 + j]), device)

    def block(d):
        return a * 4 + mod4(b + d)

    def other_block():
        return b * 4 + a

    def rows_at(d):
        return pl.ds(mod4(a + d) * 4, 4)

    def reduce_second():
        for j in range(3):
            landed(ring2.at[j], misc_sem.at[RING2 + j])
        total = (quarter[a] + ring2[0]) + (ring2[1] + ring2[2])
        sum16[...] = total.astype(jnp.bfloat16)
        for j, device in enumerate(cross_a + [sibling]):
            remote(lambda j=j: (sum16, half16.at[other, other_block()], misc_sem.at[AG1 + j]), device)

    def gather_second():
        for j, d in enumerate((1, -1, 2, 0)):
            landed(half16.at[core, block(-d)], misc_sem.at[AG1 + j])
        for j, device in enumerate(along_a):
            remote(lambda j=j: (half16.at[core, rows_at(0)], half16.at[core, rows_at(0)], misc_sem.at[AG2 + j]), device)

    def share_sib():
        for j, d in enumerate((1, -1, 2)):
            landed(half16.at[core, rows_at(-d)], misc_sem.at[AG2 + j])
        remote(lambda: (half16.at[core], half16.at[core], misc_sem.at[SIB_HALF]), sibling)

    def form_grads():
        landed(half16.at[other], misc_sem.at[SIB_HALF])
        cotangent16 = half16[0].reshape(TOKENS, RANK)
        input16 = half16[1].reshape(TOKENS, RANK)
        grad_down = SCALE * dot(hidden[...], cotangent16, 1, 0)
        grad_up = SCALE * dot(input16, buf[me], 0, 0).T
        for q in range(4):
            last = min(DOWN_ROWS, HIDDEN - q * DOWN_ROWS)
            grads[q, 0:last] = grad_down[q * DOWN_ROWS : q * DOWN_ROWS + last]
            if last < DOWN_ROWS:
                grads[q, last:DOWN_ROWS] = jnp.zeros((DOWN_ROWS - last, RANK), jnp.float32)
            grads[q, DOWN_ROWS:STEP_ROWS] = grad_up[q * UP_ROWS : (q + 1) * UP_ROWS]
        for j, (d, device) in enumerate(zip((1, -1, 2), along_y)):
            remote(lambda j=j, d=d: (grads.at[mod4(dp + d)], grads_in.at[j], misc_sem.at[Y_GRAD + j]), device)
        acc[...] += dot(down16[...], cotangent16 * jnp.bfloat16(SCALE), 1, 1)

    def share_inverse():
        remote(lambda: (inverse.at[core], inverse.at[core], misc_sem.at[SIB_INV]), sibling)

    def solve():
        for j in range(3):
            landed(grads_in.at[j], misc_sem.at[Y_GRAD + j])
        total = RATE * ((grads[dp] + grads_in[0]) + (grads_in[1] + grads_in[2]))
        landed(inverse.at[other], misc_sem.at[SIB_INV])
        step_rows = dot(total[0:DOWN_ROWS], inverse[0], 1, 0, HIGHEST)
        steps[dp, 0:DOWN_ROWS] = step_rows.astype(jnp.bfloat16)
        step_rows = dot(total[DOWN_ROWS:STEP_ROWS], inverse[1], 1, 0, HIGHEST)
        steps[dp, DOWN_ROWS:STEP_ROWS] = step_rows.astype(jnp.bfloat16)
        for j, device in enumerate(along_y):
            remote(lambda j=j: (steps.at[dp], steps.at[dp], misc_sem.at[Y_STEP + j]), device)

    def receive_chunk(k, c):
        da, db = ORDER[k]
        arrived(own[k], c)
        if db == 0 and da == -1 and c == 0:
            pass_on(own[k], c, a_plus)
        if db == 0 and da == 1 and c == 1:
            pass_on(own[k], c, a_minus)
        if db == -1 and c == 0:
            pass_on(own[k], c, b_plus)
        if db == 1 and c == 1:
            pass_on(own[k], c, b_minus)
        if db == 0:
            pass_on(own[k], c, b_plus)
            pass_on(own[k], c, b_minus)
        pass_on(own[k], c, sibling)

    def receive(*blocks):
        for k in blocks:
            for c in range(CHUNKS):
                receive_chunk(k, c)

    stores = []

    def keep(make):
        stores.append(make)
        make().start()

    def finish_steps():
        for j, d in enumerate((1, -1, 2)):
            landed(steps.at[mod4(dp - d)], misc_sem.at[Y_STEP + j])
        step_down[...] = steps[:, 0:DOWN_ROWS, :].astype(jnp.float32).reshape(4 * DOWN_ROWS, RANK)
        keep(lambda: local(step_down.at[pl.ds(0, HIDDEN)], step_down_hbm, CHUNKS))
        step_up[...] = steps[:, DOWN_ROWS:STEP_ROWS, :].astype(jnp.float32).reshape(COLS, RANK).T
        keep(lambda: local(step_up, step_up_hbm, CHUNKS + 1))

    loads[4].wait()
    schedule = {
        1: [gram_first],
        2: [lambda: receive(1, 2)],
        4: [reduce_first],
        6: [lambda: receive(3)],
        7: [gram_second],
        8: [lambda: receive(4, 5), reduce_second],
        10: [gram_third],
        11: [gather_second],
        12: [lambda: receive(6, 7)],
        14: [share_sib],
        16: [lambda: receive(8, 9), form_grads],
        20: [lambda: receive(10)],
        22: [lambda: receive(11, 12)],
        26: [share_inverse, lambda: receive(13)],
        27: [solve],
        28: [lambda: receive(14)],
    }

    def pick(values, i):
        index = values[0]
        for k in range(1, len(values)):
            index = jnp.where(i == k, values[k], index)
        return index

    def columns(slot):
        return pl.ds(pl.multiple_of(slot * COLS, COLS), COLS)

    def step(i, carry):
        for k, events in schedule.items():

            @pl.when(i == k)
            def _(events=events):
                for event in events:
                    event()

        slot = pick([(own, theirs)[who][k] for who, k in PRODUCTS], i)
        from_other = pick([who for who, _ in PRODUCTS], i)

        @pl.when(from_other == 1)
        def _():
            for c in range(CHUNKS):
                arrived(slot, c)

        def multiply():
            acc[...] += dot(weight[:, columns(slot)], buf[slot], 1, 1)

        inverting = (i >= INVERT_FROM) & (i < INVERT_TO)

        @pl.when(inverting)
        def _():
            inverse[core] = eliminate(inverse[core], 8)
            multiply()

        @pl.when(jnp.logical_not(inverting))
        def _():
            multiply()

        return carry

    lax.fori_loop(0, len(PRODUCTS), step, 0)

    slot_own, slot_sib = own[LAST], theirs[LAST]
    for c in range(CHUNKS):
        arrived(slot_own, c)
        pass_on(slot_own, c, sibling)
    for c in range(CHUNKS):
        tokens = pl.ds(c * CHUNK, CHUNK)
        acc[:, tokens] += dot(weight[:, columns(slot_own)], buf[slot_own, tokens], 1, 1)
    for c in range(CHUNKS):
        tokens = pl.ds(c * CHUNK, CHUNK)
        arrived(slot_sib, c)
        last = dot(weight[:, columns(slot_sib)], buf[slot_sib, tokens], 1, 1)
        out16[:, tokens] = (acc[:, tokens] + last).astype(jnp.bfloat16)
        keep(lambda tokens=tokens, c=c: local(out16.at[:, tokens], out_hbm.at[:, tokens], c))
    finish_steps()
    for make in pending:
        make(sibling).wait_send()
    for make in stores:
        make().wait()


def copy_kernel(*refs):
    for source, target in zip(refs[:3], refs[3:]):
        target[...] = source[...]


def per_device(hidden_input, output_gradient, frozen_weight, adapter_down, adapter_up):
    f32, bf16 = jnp.float32, jnp.bfloat16
    any_space = pl.BlockSpec(memory_space=pl.ANY)
    results = pl.pallas_call(
        kernel,
        out_shape=(
            jax.ShapeDtypeStruct((HIDDEN, TOKENS), bf16),
            jax.ShapeDtypeStruct((HIDDEN, RANK), f32),
            jax.ShapeDtypeStruct((RANK, COLS), f32),
        ),
        in_specs=[any_space] * 5,
        out_specs=(any_space,) * 3,
        scratch_shapes=[
            pltpu.VMEM((SLOTS, TOKENS, COLS), bf16),
            pltpu.VMEM((HIDDEN, SLOTS * COLS), bf16),
            pltpu.VMEM((HIDDEN, TOKENS), bf16),
            pltpu.VMEM((HIDDEN, RANK), f32),
            pltpu.VMEM((RANK, COLS), f32),
            pltpu.VMEM((HIDDEN, RANK), bf16),
            pltpu.VMEM((HIDDEN, TOKENS), f32),
            pltpu.VMEM((HIDDEN, TOKENS), bf16),
            pltpu.VMEM((2, 16, BLOCK, RANK), f32),
            pltpu.VMEM((16, BLOCK, RANK), f32),
            pltpu.VMEM((16, BLOCK, RANK), f32),
            pltpu.VMEM((4, 4, BLOCK, RANK), f32),
            pltpu.VMEM((4, BLOCK, RANK), f32),
            pltpu.VMEM((3, BLOCK, RANK), f32),
            pltpu.VMEM((64, RANK), bf16),
            pltpu.VMEM((2, 16, 64, RANK), bf16),
            pltpu.VMEM((2, 4, GRAM_ROWS, RANK), f32),
            pltpu.VMEM((GRAM_ROWS, RANK), f32),
            pltpu.VMEM((2, GRAM_ROWS, RANK), f32),
            pltpu.VMEM((2, 4, GRAM_ROWS, RANK), f32),
            pltpu.VMEM((4, GRAM_ROWS, RANK), f32),
            pltpu.VMEM((2, RANK, RANK), f32),
            pltpu.VMEM((4, STEP_ROWS, RANK), f32),
            pltpu.VMEM((3, STEP_ROWS, RANK), f32),
            pltpu.VMEM((4, STEP_ROWS, RANK), bf16),
            pltpu.VMEM((4 * DOWN_ROWS, RANK), f32),
            pltpu.VMEM((RANK, COLS), f32),
            pltpu.SemaphoreType.DMA((CHUNKS + 5,)),
            pltpu.SemaphoreType.DMA((128,)),
            pltpu.SemaphoreType.DMA((SLOTS, CHUNKS)),
            pltpu.SemaphoreType.DMA((35,)),
        ],
        compiler_params=pltpu.CompilerParams(
            collective_id=0, has_side_effects=True, vmem_limit_bytes=60 * 2**20
        ),
    )(hidden_input.T, output_gradient, frozen_weight, adapter_down, adapter_up)
    specs = (
        pl.BlockSpec((HIDDEN, COLS), lambda i: (0, i)),
        pl.BlockSpec((DOWN_ROWS, RANK), lambda i: (i, 0)),
        pl.BlockSpec((RANK, COLS), lambda i: (0, 0)),
    )
    input_grad, step_down, step_up = pl.pallas_call(
        copy_kernel,
        grid=(4,),
        out_shape=tuple(jax.ShapeDtypeStruct(r.shape, r.dtype) for r in results),
        in_specs=specs,
        out_specs=specs,
    )(*results)
    return input_grad.T, step_down, step_up


def solution(mesh):
    in_specs = (
        P("dp", "tensor"),
        P("dp", "tensor"),
        P("tensor", None),
        P("tensor", None),
        P(None, "tensor"),
    )
    out_specs = (P("dp", "tensor"), P("tensor", None), P(None, "tensor"))
    return jax.shard_map(
        per_device, mesh=mesh, in_specs=in_specs, out_specs=out_specs, check_vma=False
    )
```

time: 104 us -> 73.4 us (0.71); the launches traced: 102 us -> 73.1 us
  Pallas kernels: 91.7 us -> 72.5 us
  local copies, waits for them, and re-layouts: 9.26 us -> 0 us
    pallas_call x1 -> x2, Pallas kernels: 91.7 us -> 72.5 us  [the longest x1 68.5 us: per_device(): pl.pallas_call(kernel, out_shape=(jax.ShapeDtypeStruct((HIDDEN, TOKENS),...]
    unnamed x7 -> x0, local copies, waits for them, and re-layouts: 5.3 us -> none
    pallas_call x1 -> x0, local copies, waits for them, and re-layouts: 3.97 us -> none  [per_device(): pl.pallas_call(kernel, out_shape=(jax.ShapeDtypeStruct((TOKENS, HIDDEN),...]
where the time goes in v2:
time: 73.4 us; the launch traced here: 73.1 us
  Pallas kernels  72.5 us (99%)
    pallas_call x1, Pallas kernels, per_device(): pl.pallas_call(kernel, out_shape=(jax.ShapeDtypeStruct((HIDDEN, TOKENS),...  68.5 us
    pallas_call x1, Pallas kernels, per_device(): pl.pallas_call(copy_kernel, grid=(4,), out_shape=tuple((jax.ShapeDtypeStr...  3.96 us

profile of v2, /device:TPU:1, one launch (start us, length us, event | category | flops | bytes accessed | tf_op | source)
XLA Modules:
  0.0 73.1 jit_solution(18087236974123261812)
XLA Ops:
  0.6 68.5 %shard_map.76 = (bf16[924,1024]{1,0:T(8,128)(2,1)}, f32[924,128]{1,0:T(8,128)}, f32[128,256]{1,0:T(8,128)}) custom-call(bf16[924,1024]{1,0:T(8,128)(2,1)} %bitcast.2, bf16[1024,256]{1,0:T(8,128)(2,1)} %grad_hbm.1, bf16[924,8192]{1,0:T(8,128)(2,1)} %weight_hbm.1, f32[924,128]{1,0:T(8,128)} %down_hbm.1, f32[128,256]{1,0:T(8,128)} %up_hbm.1), custom_call_target="tpu_custom_call" | custom-call | tf_op jit(solution)/shard_map/pallas_call | solution.py:411
  69.2 4.0 %shard_map.77 = (bf16[924,1024]{1,0:T(8,128)(2,1)}, f32[924,128]{1,0:T(8,128)}, f32[128,256]{1,0:T(8,128)}) custom-call(bf16[924,1024]{1,0:T(8,128)(2,1)} %get-tuple-element.9.refs_0_, f32[924,128]{1,0:T(8,128)} %get-tuple-element.10.refs_1_, f32[128,256]{1,0:T(8,128)} %get-tuple-element.11.refs_2_), custom_call_target="tpu_custom_call" | custom-call | tf_op jit(solution)/shard_map/pallas_call | solution.py:462

commit v3 on v2

--- a/solution.py
+++ b/solution.py
@@ -23,12 +23,12 @@
 HIGHEST = lax.Precision.HIGHEST
 
 ORDER = (
-    (0, 0), (-1, 0), (1, 0), (2, 0), (0, -1), (0, 1), (-1, -1), (-1, 1), (1, -1), (1, 1),
+    (0, 0), (-1, 0), (1, 0), (0, -1), (0, 1), (2, 0), (-1, -1), (-1, 1), (1, -1), (1, 1),
     (0, 2), (2, -1), (2, 1), (-1, 2), (1, 2), (2, 2),
 )
 LAST = 15
 PRODUCTS = (
-    (0, 0), (1, 0), (0, 1), (0, 2), (1, 1), (1, 2), (0, 3), (1, 3), (0, 4), (0, 5), (1, 4), (1, 5),
+    (0, 0), (1, 0), (0, 1), (0, 2), (1, 1), (1, 2), (0, 3), (0, 4), (1, 3), (1, 4), (0, 5), (1, 5),
     (0, 6), (0, 7), (1, 6), (1, 7), (0, 8), (0, 9), (1, 8), (1, 9), (0, 10), (1, 10),
     (0, 11), (0, 12), (1, 11), (1, 12), (0, 13), (1, 13), (0, 14), (1, 14),
 )
@@ -61,11 +61,11 @@
 
 def kernel(
     hidden_hbm, grad_hbm, weight_hbm, down_hbm, up_hbm,
-    out_hbm, step_down_hbm, step_up_hbm,
-    buf, weight, hidden, down, up, down16, acc, out16,
+    out16, step_down, step_up,
+    buf, weight, hidden, down, up, down16, acc,
     part, from_sib, chip_sum, ring1, quarter, ring2, sum16, half16,
     gram_part, gram_sib, gram_sum, gram_in, gram,
-    inverse, grads, grads_in, steps, step_down, step_up,
+    inverse, grads, grads_in, steps,
     local_sem, send_sem, slot_sem, misc_sem,
 ):
     dp = lax.axis_index("dp")
@@ -199,6 +199,8 @@
 
     def gram_first():
         gram_stage(1, gram_total(0))
+
+    def own_second():
         for c in range(CHUNKS):
             pass_on(me, c, b_plus)
             pass_on(me, c, b_minus)
@@ -303,33 +305,26 @@
             for c in range(CHUNKS):
                 receive_chunk(k, c)
 
-    stores = []
-
-    def keep(make):
-        stores.append(make)
-        make().start()
-
     def finish_steps():
         for j, d in enumerate((1, -1, 2)):
             landed(steps.at[mod4(dp - d)], misc_sem.at[Y_STEP + j])
-        step_down[...] = steps[:, 0:DOWN_ROWS, :].astype(jnp.float32).reshape(4 * DOWN_ROWS, RANK)
-        keep(lambda: local(step_down.at[pl.ds(0, HIDDEN)], step_down_hbm, CHUNKS))
+        rows = steps[:, 0:DOWN_ROWS, :].astype(jnp.float32).reshape(4 * DOWN_ROWS, RANK)
+        step_down[...] = rows[0:HIDDEN]
         step_up[...] = steps[:, DOWN_ROWS:STEP_ROWS, :].astype(jnp.float32).reshape(COLS, RANK).T
-        keep(lambda: local(step_up, step_up_hbm, CHUNKS + 1))
 
     loads[4].wait()
     schedule = {
-        1: [gram_first],
-        2: [lambda: receive(1, 2)],
-        4: [reduce_first],
-        6: [lambda: receive(3)],
+        1: [own_second],
+        2: [gram_first, lambda: receive(1, 2)],
+        5: [reduce_first],
+        6: [lambda: receive(3, 4)],
         7: [gram_second],
-        8: [lambda: receive(4, 5), reduce_second],
-        10: [gram_third],
-        11: [gather_second],
-        12: [lambda: receive(6, 7)],
-        14: [share_sib],
-        16: [lambda: receive(8, 9), form_grads],
+        9: [reduce_second],
+        10: [lambda: receive(5), gram_third],
+        12: [gather_second, lambda: receive(6, 7)],
+        15: [share_sib],
+        16: [lambda: receive(8, 9)],
+        17: [form_grads],
         20: [lambda: receive(10)],
         22: [lambda: receive(11, 12)],
         26: [share_inverse, lambda: receive(13)],
@@ -338,24 +333,38 @@
     }
 
     def pick(values, i):
-        index = values[0]
-        for k in range(1, len(values)):
-            index = jnp.where(i == k, values[k], index)
-        return index
+        if len(values) == 1:
+            return values[0]
+        half = 1 << ((len(values) - 1).bit_length() - 1)
+        return jnp.where(i < half, pick(values[:half], i), pick(values[half:], i - half))
+
+    def run_events(i, keys):
+        if len(keys) == 1:
+
+            @pl.when(i == keys[0])
+            def _():
+                for event in schedule[keys[0]]:
+                    event()
+
+            return
+        half = len(keys) // 2
+
+        @pl.when(i < keys[half])
+        def _():
+            run_events(i, keys[:half])
+
+        @pl.when(i >= keys[half])
+        def _():
+            run_events(i, keys[half:])
 
     def columns(slot):
         return pl.ds(pl.multiple_of(slot * COLS, COLS), COLS)
 
     def step(i, carry):
-        for k, events in schedule.items():
-
-            @pl.when(i == k)
-            def _(events=events):
-                for event in events:
-                    event()
-
-        slot = pick([(own, theirs)[who][k] for who, k in PRODUCTS], i)
-        from_other = pick([who for who, _ in PRODUCTS], i)
+        run_events(i, sorted(schedule))
+        code = pick([(own, theirs)[who][k] + SLOTS * who for who, k in PRODUCTS], i)
+        from_other = code // SLOTS
+        slot = code - SLOTS * from_other
 
         @pl.when(from_other == 1)
         def _():
@@ -392,31 +401,23 @@
         arrived(slot_sib, c)
         last = dot(weight[:, columns(slot_sib)], buf[slot_sib, tokens], 1, 1)
         out16[:, tokens] = (acc[:, tokens] + last).astype(jnp.bfloat16)
-        keep(lambda tokens=tokens, c=c: local(out16.at[:, tokens], out_hbm.at[:, tokens], c))
     finish_steps()
     for make in pending:
         make(sibling).wait_send()
-    for make in stores:
-        make().wait()
-
-
-def copy_kernel(*refs):
-    for source, target in zip(refs[:3], refs[3:]):
-        target[...] = source[...]
 
 
 def per_device(hidden_input, output_gradient, frozen_weight, adapter_down, adapter_up):
     f32, bf16 = jnp.float32, jnp.bfloat16
     any_space = pl.BlockSpec(memory_space=pl.ANY)
-    results = pl.pallas_call(
+    input_grad, step_down, step_up = pl.pallas_call(
         kernel,
         out_shape=(
-            jax.ShapeDtypeStruct((HIDDEN, TOKENS), bf16),
-            jax.ShapeDtypeStruct((HIDDEN, RANK), f32),
-            jax.ShapeDtypeStruct((RANK, COLS), f32),
+            pltpu.VMEM((HIDDEN, TOKENS), bf16),
+            pltpu.VMEM((HIDDEN, RANK), f32),
+            pltpu.VMEM((RANK, COLS), f32),
         ),
         in_specs=[any_space] * 5,
-        out_specs=(any_space,) * 3,
+        out_specs=(pl.BlockSpec(memory_space=pltpu.VMEM),) * 3,
         scratch_shapes=[
             pltpu.VMEM((SLOTS, TOKENS, COLS), bf16),
             pltpu.VMEM((HIDDEN, SLOTS * COLS), bf16),
@@ -425,7 +426,6 @@
             pltpu.VMEM((RANK, COLS), f32),
             pltpu.VMEM((HIDDEN, RANK), bf16),
             pltpu.VMEM((HIDDEN, TOKENS), f32),
-            pltpu.VMEM((HIDDEN, TOKENS), bf16),
             pltpu.VMEM((2, 16, BLOCK, RANK), f32),
             pltpu.VMEM((16, BLOCK, RANK), f32),
             pltpu.VMEM((16, BLOCK, RANK), f32),
@@ -443,29 +443,15 @@
             pltpu.VMEM((4, STEP_ROWS, RANK), f32),
             pltpu.VMEM((3, STEP_ROWS, RANK), f32),
             pltpu.VMEM((4, STEP_ROWS, RANK), bf16),
-            pltpu.VMEM((4 * DOWN_ROWS, RANK), f32),
-            pltpu.VMEM((RANK, COLS), f32),
             pltpu.SemaphoreType.DMA((CHUNKS + 5,)),
             pltpu.SemaphoreType.DMA((128,)),
             pltpu.SemaphoreType.DMA((SLOTS, CHUNKS)),
             pltpu.SemaphoreType.DMA((35,)),
         ],
         compiler_params=pltpu.CompilerParams(
-            collective_id=0, has_side_effects=True, vmem_limit_bytes=60 * 2**20
+            collective_id=0, has_side_effects=True, vmem_limit_bytes=52 * 2**20
         ),
     )(hidden_input.T, output_gradient, frozen_weight, adapter_down, adapter_up)
-    specs = (
-        pl.BlockSpec((HIDDEN, COLS), lambda i: (0, i)),
-        pl.BlockSpec((DOWN_ROWS, RANK), lambda i: (i, 0)),
-        pl.BlockSpec((RANK, COLS), lambda i: (0, 0)),
-    )
-    input_grad, step_down, step_up = pl.pallas_call(
-        copy_kernel,
-        grid=(4,),
-        out_shape=tuple(jax.ShapeDtypeStruct(r.shape, r.dtype) for r in results),
-        in_specs=specs,
-        out_specs=specs,
-    )(*results)
     return input_grad.T, step_down, step_up
 
 

time: 73.4 us -> 67 us (0.913)
  Pallas kernels: 72.5 us -> 63.5 us
  local copies, waits for them, and re-layouts: 0 us -> 2.68 us
    pallas_call x2 -> x1, Pallas kernels: 72.5 us -> 63.5 us  [per_device(): pl.pallas_call(kernel, out_shape=(pltpu.VMEM((HIDDEN, TOKENS), bf16), plt...]
    unnamed x0 -> x3, local copies, waits for them, and re-layouts: none -> 2.68 us
where the time goes in v3:
time: 67 us; the launch traced here: 66.8 us
  Pallas kernels  63.5 us (95%)
  local copies, waits for them, and re-layouts  2.68 us (4%)
    pallas_call x1, Pallas kernels, per_device(): pl.pallas_call(kernel, out_shape=(pltpu.VMEM((HIDDEN, TOKENS), bf16), plt...  63.5 us
    unnamed x3, local copies, waits for them, and re-layouts  2.68 us

profile of v3, /device:TPU:1, one launch (start us, length us, event | category | flops | bytes accessed | tf_op | source)
XLA Modules:
  0.0 66.8 jit_solution(1292429648548766375)
XLA Ops:
  0.6 63.5 %shard_map.76 = (bf16[924,1024]{1,0:T(8,128)(2,1)S(1)}, f32[924,128]{1,0:T(8,128)S(1)}, f32[128,256]{1,0:T(8,128)S(1)}) custom-call(bf16[924,1024]{1,0:T(8,128)(2,1)} %bitcast.3, bf16[1024,256]{1,0:T(8,128)(2,1)} %grad_hbm.1, bf16[924,8192]{1,0:T(8,128)(2,1)} %weight_hbm.1, f32[924,128]{1,0:T(8,128)} %down_hbm.1, f32[128,256]{1,0:T(8,128)} %up_hbm.1), custom_call_target="tpu_custom_call" | custom-call | tf_op jit(solution)/shard_map/pallas_call | solution.py:412
  64.1 1.3 %copy.11 = bf16[1024,924]{0,1:T(8,128)(2,1)} copy(bf16[1024,924]{0,1:T(8,128)(2,1)S(1)} %bitcast.2) | data formatting | bytes 3784704
  65.4 0.7 copy.13
  66.1 0.8 %copy.12 = f32[924,128]{1,0:T(8,128)} copy(f32[924,128]{1,0:T(8,128)S(1)} %get-tuple-element.10) | data formatting | bytes 946176

commit v4 on v3

--- a/solution.py
+++ b/solution.py
@@ -32,7 +32,7 @@
     (0, 6), (0, 7), (1, 6), (1, 7), (0, 8), (0, 9), (1, 8), (1, 9), (0, 10), (1, 10),
     (0, 11), (0, 12), (1, 11), (1, 12), (0, 13), (1, 13), (0, 14), (1, 14),
 )
-INVERT_FROM, INVERT_TO = 10, 26
+INVERT_FROM, INVERT_TO = 9, 25
 
 
 def dot(left, right, dims_left, dims_right, precision=None):
@@ -103,9 +103,6 @@
         local(down_hbm, down, 3),
         local(weight_hbm, weight, 4),
     ]
-    for load in loads[:4]:
-        load.start()
-
     barrier = pltpu.get_barrier_semaphore()
     cross_a = [(dp, place(other, b, a + d)) for d in (1, -1, 2)]
     cross_b = [(dp, place(other, b + d, a)) for d in (1, -1, 2)]
@@ -113,7 +110,16 @@
     for partner in partners:
         pl.semaphore_signal(barrier, inc=1, device_id=partner, device_id_type=MESH)
 
+    for load in loads[:4]:
+        load.start()
+
     pending = []
+    drained = [0]
+    marks = {}
+
+    def mark(name):
+        marks[name] = len(pending)
+
 
     def remote(refs, device):
         index = len(pending)
@@ -132,6 +138,11 @@
         pending.append(make)
         make(device).start()
 
+    def drain(until):
+        while drained[0] < until:
+            pending[drained[0]](sibling).wait_send()
+            drained[0] += 1
+
     def landed(dst, recv_sem):
         pltpu.make_async_remote_copy(
             src_ref=dst,
@@ -148,6 +159,9 @@
     def pass_on(slot, c, device):
         remote(lambda: (piece(slot, c), piece(slot, c), slot_sem.at[slot, c]), device)
 
+    def hand_over(slot):
+        remote(lambda: (buf.at[slot], buf.at[slot], slot_sem.at[slot, 0]), sibling)
+
     def arrived(slot, c):
         landed(piece(slot, c), slot_sem.at[slot, c])
 
@@ -163,20 +177,19 @@
     up_f32 = up[...]
     part[0] = dot(buf[me], up_f32.astype(jnp.bfloat16), 1, 1).reshape(16, BLOCK, RANK)
     gram_part[0] = dot(up_f32, up_f32, 1, 1, HIGHEST).reshape(4, GRAM_ROWS, RANK)
+    pl.semaphore_wait(barrier, len(partners))
+    own_first(0)
+    own_first(1)
     loads[2].wait()
     loads[3].wait()
     loads[4].start()
     down_f32 = down[...]
     down16[...] = down_f32.astype(jnp.bfloat16)
     gram_part[1] = dot(down_f32, down_f32, 0, 0, HIGHEST).reshape(4, GRAM_ROWS, RANK)
+    remote(lambda: (gram_part.at[other, dp], gram_sib, misc_sem.at[GRAM_SIB]), sibling)
     part[1] = dot(down16[...], hidden[...], 0, 0).T.reshape(16, BLOCK, RANK)
-    pl.semaphore_wait(barrier, len(partners))
-    remote(lambda: (gram_part.at[other, dp], gram_sib, misc_sem.at[GRAM_SIB]), sibling)
     remote(lambda: (part.at[other], from_sib, misc_sem.at[SIB_PART]), sibling)
-    own_first(0)
-    own_first(1)
-    for c in range(CHUNKS):
-        pass_on(me, c, sibling)
+    hand_over(me)
     acc[...] = jnp.zeros_like(acc)
 
     def gram_stage(n, value):
@@ -200,10 +213,11 @@
     def gram_first():
         gram_stage(1, gram_total(0))
 
-    def own_second():
-        for c in range(CHUNKS):
-            pass_on(me, c, b_plus)
-            pass_on(me, c, b_minus)
+    mark("first")
+
+    def own_second(c):
+        pass_on(me, c, b_plus)
+        pass_on(me, c, b_minus)
 
     def gram_second():
         gram[dp] = gram_total(1)
@@ -298,12 +312,13 @@
         if db == 0:
             pass_on(own[k], c, b_plus)
             pass_on(own[k], c, b_minus)
-        pass_on(own[k], c, sibling)
 
     def receive(*blocks):
-        for k in blocks:
-            for c in range(CHUNKS):
+        for c in range(CHUNKS):
+            for k in blocks:
                 receive_chunk(k, c)
+                if c == CHUNKS - 1:
+                    hand_over(own[k])
 
     def finish_steps():
         for j, d in enumerate((1, -1, 2)):
@@ -314,21 +329,22 @@
 
     loads[4].wait()
     schedule = {
-        1: [own_second],
+        0: [lambda: own_second(0)],
+        1: [lambda: own_second(1)],
         2: [gram_first, lambda: receive(1, 2)],
         5: [reduce_first],
-        6: [lambda: receive(3, 4)],
+        6: [lambda: mark("second"), lambda: drain(marks["first"]), lambda: receive(3, 4)],
         7: [gram_second],
-        9: [reduce_second],
-        10: [lambda: receive(5), gram_third],
+        9: [reduce_second, gram_third],
+        10: [lambda: receive(5)],
         12: [gather_second, lambda: receive(6, 7)],
-        15: [share_sib],
+        15: [lambda: mark("third"), lambda: drain(marks["second"]), share_sib],
         16: [lambda: receive(8, 9)],
         17: [form_grads],
         20: [lambda: receive(10)],
         22: [lambda: receive(11, 12)],
-        26: [share_inverse, lambda: receive(13)],
-        27: [solve],
+        25: [share_inverse],
+        26: [lambda: receive(13), lambda: drain(marks["third"]), solve],
         28: [lambda: receive(14)],
     }
 
@@ -368,8 +384,7 @@
 
         @pl.when(from_other == 1)
         def _():
-            for c in range(CHUNKS):
-                arrived(slot, c)
+            landed(buf.at[slot], slot_sem.at[slot, 0])
 
         def multiply():
             acc[...] += dot(weight[:, columns(slot)], buf[slot], 1, 1)
@@ -402,8 +417,7 @@
         last = dot(weight[:, columns(slot_sib)], buf[slot_sib, tokens], 1, 1)
         out16[:, tokens] = (acc[:, tokens] + last).astype(jnp.bfloat16)
     finish_steps()
-    for make in pending:
-        make(sibling).wait_send()
+    drain(len(pending))
 
 
 def per_device(hidden_input, output_gradient, frozen_weight, adapter_down, adapter_up):

time: 67 us -> 66.8 us (level)
  no operation moved by 1% of the time
where the time goes in v4:
time: 66.8 us; the launch traced here: 66.7 us
  Pallas kernels  63.4 us (95%)
  local copies, waits for them, and re-layouts  2.68 us (4%)
    pallas_call x1, Pallas kernels, per_device(): pl.pallas_call(kernel, out_shape=(pltpu.VMEM((HIDDEN, TOKENS), bf16), plt...  63.4 us
    unnamed x3, local copies, waits for them, and re-layouts  2.68 us

profile of v4, /device:TPU:1, one launch (start us, length us, event | category | flops | bytes accessed | tf_op | source)
XLA Modules:
  0.0 66.7 jit_solution(15570426919567321917)
XLA Ops:
  0.6 63.4 %shard_map.76 = (bf16[924,1024]{1,0:T(8,128)(2,1)S(1)}, f32[924,128]{1,0:T(8,128)S(1)}, f32[128,256]{1,0:T(8,128)S(1)}) custom-call(bf16[924,1024]{1,0:T(8,128)(2,1)} %bitcast.3, bf16[1024,256]{1,0:T(8,128)(2,1)} %grad_hbm.1, bf16[924,8192]{1,0:T(8,128)(2,1)} %weight_hbm.1, f32[924,128]{1,0:T(8,128)} %down_hbm.1, f32[128,256]{1,0:T(8,128)} %up_hbm.1), custom_call_target="tpu_custom_call" | custom-call | tf_op jit(solution)/shard_map/pallas_call | solution.py:426
  64.0 1.3 %copy.11 = bf16[1024,924]{0,1:T(8,128)(2,1)} copy(bf16[1024,924]{0,1:T(8,128)(2,1)S(1)} %bitcast.2) | data formatting | bytes 3784704
  65.2 0.7 copy.13
  65.9 0.8 %copy.12 = f32[924,128]{1,0:T(8,128)} copy(f32[924,128]{1,0:T(8,128)S(1)} %get-tuple-element.10) | data formatting | bytes 946176
